TPU v7x, 256 devices: a whole 4x4x8 slice. The times are simulated.
256 devices in a mesh: layer: 8 (over y, core), expert: 32 (over z, x).
Axes of the slice: x: 4, y: 4, z: 8, core: 2. Of those that a mesh axis runs over, the one named last changes fastest.
Arguments:
- stream_in: bfloat16 [4, 1024, 3584], P(None, 'expert'), may hold values from -6 to 6
- gain: float32 [8, 3584], P('layer'), may hold values from 0.5 to 1.5
- w_gate: bfloat16 [8, 3584, 8192], P('layer', None, 'expert'), may hold values from -0.09375 to 0.09375
- w_up: bfloat16 [8, 3584, 8192], P('layer', None, 'expert'), may hold values from -0.09375 to 0.09375
- w_down: bfloat16 [8, 8192, 3584], P('layer', 'expert'), may hold values from -0.125 to 0.125
- routes: int32 [8, 4, 1024, 8], P('layer', None, 'expert'), may hold values from 0 to 255, all different within a row; in each aligned block of 32 rows (0 to 31, 32 to 63, ..., all dimensions but the last counted through in order) at most 2 rows name the same one
- gates: float32 [8, 4, 1024, 8], P('layer', None, 'expert'), may hold values from 0.2 to 1
Outputs:
- layer_out: bfloat16 [8, 4, 1024, 3584], P('layer', None, 'expert')
- hessian: float32 [8, 8192, 2048], P('layer', 'expert')
Inputs may be any that keep to these rules, and one draw needn't show every extreme that they name: `routes`: each token names 8 different experts; in each aligned block of 32 tokens (the rows of one device) no expert is named by more than 2 tokens.
All inputs are finite; a program needn't handle non-finite values.
Results may differ from a plain program's by a relative error of at most 0.014.
Values may be sent and summed in bfloat16 or wider, within the bound.
A program may use at most 64 MiB of HBM per device.

v0:
```python
import jax
import jax.numpy as jnp
from jax import lax
from jax.sharding import PartitionSpec as P

GROUP = 8
CAP = 2


EPSILON = 1e-06


def partner(value, axis, bit):
    return lax.ppermute(value, axis, [(i, i ^ 1 << bit) for i in range(lax.axis_size(axis))])


def passed_along(value, axis, by):
    devices = lax.axis_size(axis)
    pairs = [(i, i + by) for i in range(devices) if 0 <= i + by < devices]
    return lax.ppermute(value, axis, pairs)


def normalize(rows, gain_row):
    wide = rows.astype(jnp.float32)
    scale = lax.rsqrt(jnp.mean(wide * wide, axis=-1, keepdims=True) + EPSILON)
    return (wide * scale * gain_row).astype(jnp.bfloat16)


def slot_tables(route_rows, gate_rows, flight, capacity):
    expert_ids = lax.broadcasted_iota(jnp.int32, (1, 1, flight), 2)
    matches = route_rows[:, :, None] == expert_ids
    routed = jnp.any(matches, axis=1)
    weight = jnp.sum(jnp.where(matches, gate_rows[:, :, None], 0.0), axis=1)
    place = jnp.cumsum(routed.astype(jnp.int32), axis=0) - 1
    slot_ids = lax.broadcasted_iota(jnp.int32, (1, 1, capacity), 2)
    select = jnp.logical_and(routed[:, :, None], place[:, :, None] == slot_ids)
    return (select.astype(jnp.bfloat16), weight)


def member_bit(bit):
    return lax.axis_index("expert") >> bit & 1


def share_units(hidden):
    joined = hidden
    for bit in range(GROUP.bit_length() - 1):
        other = partner(joined, "expert", bit)
        upper = member_bit(bit) == 1
        joined = jnp.where(
            upper,
            jnp.concatenate([other, joined], axis=1),
            jnp.concatenate([joined, other], axis=1),
        )
    return joined


def layer_step(current, gain_row, gate_weight, up_weight, down_weight, route_rows, gate_rows):
    devices = lax.axis_size("expert")
    flight = devices // GROUP
    width = current.shape[1]
    normed = normalize(current, gain_row)
    select, weight = slot_tables(route_rows, gate_rows, flight, CAP)
    outbound = jnp.einsum("tfc,td->fcd", select, normed, preferred_element_type=jnp.float32).astype(
        jnp.bfloat16
    )
    outbound = jnp.broadcast_to(outbound[:, None], (flight, GROUP, CAP, width)).reshape(
        devices, CAP, width
    )
    arrived = lax.all_to_all(outbound, "expert", split_axis=0, concat_axis=0, tiled=True)
    rows = arrived.reshape(devices * CAP, width)
    gate_act = jnp.dot(rows, gate_weight, preferred_element_type=jnp.float32)
    up_act = jnp.dot(rows, up_weight, preferred_element_type=jnp.float32)
    hidden = (jax.nn.silu(gate_act) * up_act).astype(jnp.bfloat16)
    every_unit = share_units(hidden)
    gram_term = lax.dot_general(
        hidden, every_unit, (((0,), (0,)), ((), ())), preferred_element_type=jnp.float32
    )
    partial_value = jnp.dot(hidden, down_weight, preferred_element_type=jnp.float32).astype(
        jnp.bfloat16
    )
    returned = lax.all_to_all(
        partial_value.reshape(devices, CAP, width),
        "expert",
        split_axis=0,
        concat_axis=0,
        tiled=True,
    )
    returned = returned.reshape(flight, GROUP, CAP, width)
    picked = jnp.einsum("tfc,fgcd->tfd", select, returned, preferred_element_type=jnp.float32)
    update = jnp.sum(weight[:, :, None] * picked, axis=1)
    following = (current.astype(jnp.float32) + update).astype(jnp.bfloat16)
    return (following, gram_term)


def shards(stream_in, gain, w_gate, w_up, w_down, routes, gates):
    fronts = stream_in.shape[0]
    tok_rows = stream_in.shape[1]
    width = stream_in.shape[2]
    units = w_gate.shape[2]
    sections = lax.axis_size("layer")
    section = lax.axis_index("layer")

    def advance(step, carry):
        incoming, produced, gram = carry
        front = step - section
        valid = jnp.logical_and(front >= 0, front < fronts)
        slot = jnp.clip(front, 0, fronts - 1)
        fresh = lax.dynamic_index_in_dim(
            stream_in, jnp.minimum(step, fronts - 1), 0, keepdims=False
        )
        current = jnp.where(section == 0, fresh, incoming)
        route_rows = lax.dynamic_index_in_dim(routes[0], slot, 0, keepdims=False)
        gate_rows = lax.dynamic_index_in_dim(gates[0], slot, 0, keepdims=False)
        following, gram_term = layer_step(
            current, gain[0], w_gate[0], w_up[0], w_down[0], route_rows, gate_rows
        )
        kept = lax.dynamic_index_in_dim(produced, slot, 0, keepdims=False)
        produced = lax.dynamic_update_index_in_dim(
            produced, jnp.where(valid, following, kept), slot, 0
        )
        gram = gram + jnp.where(valid, gram_term, 0.0)
        incoming = passed_along(following, "layer", 1)
        return (incoming, produced, gram)

    start = (
        jnp.zeros((tok_rows, width), jnp.bfloat16),
        jnp.zeros((fronts, tok_rows, width), jnp.bfloat16),
        jnp.zeros((units, GROUP * units), jnp.float32),
    )
    incoming, produced, gram = lax.fori_loop(0, fronts + sections - 1, advance, start)
    return (produced[None], (gram * (1.0 / (fronts * CAP)))[None])


def solution(mesh):
    return jax.shard_map(
        shards,
        mesh=mesh,
        in_specs=(
            P(None, "expert", None),
            P("layer", None),
            P("layer", None, "expert"),
            P("layer", None, "expert"),
            P("layer", "expert", None),
            P("layer", None, "expert", None),
            P("layer", None, "expert", None),
        ),
        out_specs=(P("layer", None, "expert", None), P("layer", "expert", None)),
        check_vma=False,
    )
```

profile of v0, /device:TPU:1, one launch (start us, length us, event | category | flops | bytes accessed | tf_op | source)
XLA Modules:
  0.0 624.3 jit_solution(8670026835223380225)
XLA Ops:
  1.7 621.1 %while.20 = (s32[]{:T(128)}, bf16[32,3584]{1,0:T(8,128)(2,1)S(1)}, bf16[4,32,3584]{2,1,0:T(8,128)(2,1)}, f32[256,2048]{1,0:T(8,128)S(1)}, pred[]{:T(512)}, /*ind...) while((s32[]{:T(128)}, bf16[32,3584]{1,0:T(8,128)(2,1)S(1)}, ...), condition=%wide.region_7.8_spmd.clone, body=%wide.region_0.7_spmd.clone.sunk | while | flops 429712800 | bytes 37135672 | solution.py:130
  5.1 26.1 %all_to_all.28 = bf16[32,2,3584]{2,1,0:T(2,128)(2,1)S(1)} all-to-all(bf16[32,2,3584]{2,1,0:T(2,128)(2,1)S(1)} %bitcast.82), channel_id=1, replica_groups=mesh['layer'=8,'expert'=32] {'expert'}, dimensions={0} | all-to-all | bytes 917504 | tf_op jit(solution)/shard_map/while/body/eval_jaxpr/all_to_all | solution.py:69
  35.3 5.7 all-to-all-start.1
  56.8 6.6 %collective-permute-start = (bf16[32,3584]{1,0:T(8,128)(2,1)S(1)}, bf16[32,3584]{1,0:T(8,128)(2,1)S(1)}, u32[]{:S(2)}, u32[]{:S(2)}) collective-permute-start(bf16[32,3584]{1,0:T(8,128)(2,1)S(1)} %get-tuple-element.454), channel_id=1, source_target_pairs={{0,32},{32,64},{64,96},{96,128},{128,160},{160,192},{192,224},{1,3... | collective-permute-start | bytes 688136 | tf_op jit(solution)/shard_map/while/body/eval_jaxpr/ppermute | solution.py:20
  69.7 20.6 %all_to_all.28 = bf16[32,2,3584]{2,1,0:T(2,128)(2,1)S(1)} all-to-all(bf16[32,2,3584]{2,1,0:T(2,128)(2,1)S(1)} %bitcast.82), channel_id=1, replica_groups=mesh['layer'=8,'expert'=32] {'expert'}, dimensions={0} | all-to-all | bytes 917504 | tf_op jit(solution)/shard_map/while/body/eval_jaxpr/all_to_all | solution.py:69
  116.5 5.4 collective-permute-start
  128.2 18.8 %all_to_all.28 = bf16[32,2,3584]{2,1,0:T(2,128)(2,1)S(1)} all-to-all(bf16[32,2,3584]{2,1,0:T(2,128)(2,1)S(1)} %bitcast.82), channel_id=1, replica_groups=mesh['layer'=8,'expert'=32] {'expert'}, dimensions={0} | all-to-all | bytes 917504 | tf_op jit(solution)/shard_map/while/body/eval_jaxpr/all_to_all | solution.py:69
  171.5 8.7 %collective-permute-start = (bf16[32,3584]{1,0:T(8,128)(2,1)S(1)}, bf16[32,3584]{1,0:T(8,128)(2,1)S(1)}, u32[]{:S(2)}, u32[]{:S(2)}) collective-permute-start(bf16[32,3584]{1,0:T(8,128)(2,1)S(1)} %get-tuple-element.454), channel_id=1, source_target_pairs={{0,32},{32,64},{64,96},{96,128},{128,160},{160,192},{192,224},{1,3... | collective-permute-start | bytes 688136 | tf_op jit(solution)/shard_map/while/body/eval_jaxpr/ppermute | solution.py:20
  186.5 17.9 %all_to_all.28 = bf16[32,2,3584]{2,1,0:T(2,128)(2,1)S(1)} all-to-all(bf16[32,2,3584]{2,1,0:T(2,128)(2,1)S(1)} %bitcast.82), channel_id=1, replica_groups=mesh['layer'=8,'expert'=32] {'expert'}, dimensions={0} | all-to-all | bytes 917504 | tf_op jit(solution)/shard_map/while/body/eval_jaxpr/all_to_all | solution.py:69
  226.3 7.1 %collective-permute-start = (bf16[32,3584]{1,0:T(8,128)(2,1)S(1)}, bf16[32,3584]{1,0:T(8,128)(2,1)S(1)}, u32[]{:S(2)}, u32[]{:S(2)}) collective-permute-start(bf16[32,3584]{1,0:T(8,128)(2,1)S(1)} %get-tuple-element.454), channel_id=1, source_target_pairs={{0,32},{32,64},{64,96},{96,128},{128,160},{160,192},{192,224},{1,3... | collective-permute-start | bytes 688136 | tf_op jit(solution)/shard_map/while/body/eval_jaxpr/ppermute | solution.py:20
  239.8 19.8 %all_to_all.28 = bf16[32,2,3584]{2,1,0:T(2,128)(2,1)S(1)} all-to-all(bf16[32,2,3584]{2,1,0:T(2,128)(2,1)S(1)} %bitcast.82), channel_id=1, replica_groups=mesh['layer'=8,'expert'=32] {'expert'}, dimensions={0} | all-to-all | bytes 917504 | tf_op jit(solution)/shard_map/while/body/eval_jaxpr/all_to_all | solution.py:69
  281.7 6.9 %collective-permute-start = (bf16[32,3584]{1,0:T(8,128)(2,1)S(1)}, bf16[32,3584]{1,0:T(8,128)(2,1)S(1)}, u32[]{:S(2)}, u32[]{:S(2)}) collective-permute-start(bf16[32,3584]{1,0:T(8,128)(2,1)S(1)} %get-tuple-element.454), channel_id=1, source_target_pairs={{0,32},{32,64},{64,96},{96,128},{128,160},{160,192},{192,224},{1,3... | collective-permute-start | bytes 688136 | tf_op jit(solution)/shard_map/while/body/eval_jaxpr/ppermute | solution.py:20
  295.0 19.8 %all_to_all.28 = bf16[32,2,3584]{2,1,0:T(2,128)(2,1)S(1)} all-to-all(bf16[32,2,3584]{2,1,0:T(2,128)(2,1)S(1)} %bitcast.82), channel_id=1, replica_groups=mesh['layer'=8,'expert'=32] {'expert'}, dimensions={0} | all-to-all | bytes 917504 | tf_op jit(solution)/shard_map/while/body/eval_jaxpr/all_to_all | solution.py:69
  336.9 6.9 %collective-permute-start = (bf16[32,3584]{1,0:T(8,128)(2,1)S(1)}, bf16[32,3584]{1,0:T(8,128)(2,1)S(1)}, u32[]{:S(2)}, u32[]{:S(2)}) collective-permute-start(bf16[32,3584]{1,0:T(8,128)(2,1)S(1)} %get-tuple-element.454), channel_id=1, source_target_pairs={{0,32},{32,64},{64,96},{96,128},{128,160},{160,192},{192,224},{1,3... | collective-permute-start | bytes 688136 | tf_op jit(solution)/shard_map/while/body/eval_jaxpr/ppermute | solution.py:20
  350.2 19.8 %all_to_all.28 = bf16[32,2,3584]{2,1,0:T(2,128)(2,1)S(1)} all-to-all(bf16[32,2,3584]{2,1,0:T(2,128)(2,1)S(1)} %bitcast.82), channel_id=1, replica_groups=mesh['layer'=8,'expert'=32] {'expert'}, dimensions={0} | all-to-all | bytes 917504 | tf_op jit(solution)/shard_map/while/body/eval_jaxpr/all_to_all | solution.py:69
  392.1 6.9 %collective-permute-start = (bf16[32,3584]{1,0:T(8,128)(2,1)S(1)}, bf16[32,3584]{1,0:T(8,128)(2,1)S(1)}, u32[]{:S(2)}, u32[]{:S(2)}) collective-permute-start(bf16[32,3584]{1,0:T(8,128)(2,1)S(1)} %get-tuple-element.454), channel_id=1, source_target_pairs={{0,32},{32,64},{64,96},{96,128},{128,160},{160,192},{192,224},{1,3... | collective-permute-start | bytes 688136 | tf_op jit(solution)/shard_map/while/body/eval_jaxpr/ppermute | solution.py:20
  405.4 19.8 %all_to_all.28 = bf16[32,2,3584]{2,1,0:T(2,128)(2,1)S(1)} all-to-all(bf16[32,2,3584]{2,1,0:T(2,128)(2,1)S(1)} %bitcast.82), channel_id=1, replica_groups=mesh['layer'=8,'expert'=32] {'expert'}, dimensions={0} | all-to-all | bytes 917504 | tf_op jit(solution)/shard_map/while/body/eval_jaxpr/all_to_all | solution.py:69
  447.3 6.9 %collective-permute-start = (bf16[32,3584]{1,0:T(8,128)(2,1)S(1)}, bf16[32,3584]{1,0:T(8,128)(2,1)S(1)}, u32[]{:S(2)}, u32[]{:S(2)}) collective-permute-start(bf16[32,3584]{1,0:T(8,128)(2,1)S(1)} %get-tuple-element.454), channel_id=1, source_target_pairs={{0,32},{32,64},{64,96},{96,128},{128,160},{160,192},{192,224},{1,3... | collective-permute-start | bytes 688136 | tf_op jit(solution)/shard_map/while/body/eval_jaxpr/ppermute | solution.py:20
  460.6 19.8 %all_to_all.28 = bf16[32,2,3584]{2,1,0:T(2,128)(2,1)S(1)} all-to-all(bf16[32,2,3584]{2,1,0:T(2,128)(2,1)S(1)} %bitcast.82), channel_id=1, replica_groups=mesh['layer'=8,'expert'=32] {'expert'}, dimensions={0} | all-to-all | bytes 917504 | tf_op jit(solution)/shard_map/while/body/eval_jaxpr/all_to_all | solution.py:69
  502.5 6.9 %collective-permute-start = (bf16[32,3584]{1,0:T(8,128)(2,1)S(1)}, bf16[32,3584]{1,0:T(8,128)(2,1)S(1)}, u32[]{:S(2)}, u32[]{:S(2)}) collective-permute-start(bf16[32,3584]{1,0:T(8,128)(2,1)S(1)} %get-tuple-element.454), channel_id=1, source_target_pairs={{0,32},{32,64},{64,96},{96,128},{128,160},{160,192},{192,224},{1,3... | collective-permute-start | bytes 688136 | tf_op jit(solution)/shard_map/while/body/eval_jaxpr/ppermute | solution.py:20
  515.8 19.8 %all_to_all.28 = bf16[32,2,3584]{2,1,0:T(2,128)(2,1)S(1)} all-to-all(bf16[32,2,3584]{2,1,0:T(2,128)(2,1)S(1)} %bitcast.82), channel_id=1, replica_groups=mesh['layer'=8,'expert'=32] {'expert'}, dimensions={0} | all-to-all | bytes 917504 | tf_op jit(solution)/shard_map/while/body/eval_jaxpr/all_to_all | solution.py:69
  557.7 6.9 %collective-permute-start = (bf16[32,3584]{1,0:T(8,128)(2,1)S(1)}, bf16[32,3584]{1,0:T(8,128)(2,1)S(1)}, u32[]{:S(2)}, u32[]{:S(2)}) collective-permute-start(bf16[32,3584]{1,0:T(8,128)(2,1)S(1)} %get-tuple-element.454), channel_id=1, source_target_pairs={{0,32},{32,64},{64,96},{96,128},{128,160},{160,192},{192,224},{1,3... | collective-permute-start | bytes 688136 | tf_op jit(solution)/shard_map/while/body/eval_jaxpr/ppermute | solution.py:20
  571.0 19.8 %all_to_all.28 = bf16[32,2,3584]{2,1,0:T(2,128)(2,1)S(1)} all-to-all(bf16[32,2,3584]{2,1,0:T(2,128)(2,1)S(1)} %bitcast.82), channel_id=1, replica_groups=mesh['layer'=8,'expert'=32] {'expert'}, dimensions={0} | all-to-all | bytes 917504 | tf_op jit(solution)/shard_map/while/body/eval_jaxpr/all_to_all | solution.py:69
  612.9 6.9 %collective-permute-start = (bf16[32,3584]{1,0:T(8,128)(2,1)S(1)}, bf16[32,3584]{1,0:T(8,128)(2,1)S(1)}, u32[]{:S(2)}, u32[]{:S(2)}) collective-permute-start(bf16[32,3584]{1,0:T(8,128)(2,1)S(1)} %get-tuple-element.454), channel_id=1, source_target_pairs={{0,32},{32,64},{64,96},{96,128},{128,160},{160,192},{192,224},{1,3... | collective-permute-start | bytes 688136 | tf_op jit(solution)/shard_map/while/body/eval_jaxpr/ppermute | solution.py:20
  (454 shorter events, 318.2 us)
Async XLA Ops:
  35.3 19.8 %all-to-all-start.1 = ((bf16[32,2,3584]{2,1,0:T(2,128)(2,1)}), bf16[32,2,3584]{2,1,0:T(2,128)(2,1)S(1)}, u32[]{:S(2)}, u32[]{:S(2)}) async-start(bf16[32,2,3584]{2,1,0:T(2,128)(2,1)} %reshape.92), calls=%async_computation.1 | async-start | bytes 917504 | tf_op jit(solution)/shard_map/while/body/eval_jaxpr/all_to_all | solution.py:81
  51.8 11.6 %collective-permute-start.3 = (bf16[64,1024]{1,0:T(8,128)(2,1)S(1)}, bf16[64,1024]{1,0:T(8,128)(2,1)S(1)}, u32[]{:S(2)}, u32[]{:S(2)}) collective-permute-start(bf16[64,1024]{1,0:T(8,128)(2,1)S(1)} %maximum_select_fusion.9), channel_id=1, source_target_pairs={{0,4},{1,5},{2,6},{3,7},{4,0},{5,1},{6,2},{7,3},{8,12},{9,13},{10,... | collective-permute-start | bytes 393224 | tf_op jit(solution)/shard_map/while/body/eval_jaxpr/ppermute | solution.py:14
  94.5 20.3 %all-to-all-start.1 = ((bf16[32,2,3584]{2,1,0:T(2,128)(2,1)}), bf16[32,2,3584]{2,1,0:T(2,128)(2,1)S(1)}, u32[]{:S(2)}, u32[]{:S(2)}) async-start(bf16[32,2,3584]{2,1,0:T(2,128)(2,1)} %reshape.92), calls=%async_computation.1 | async-start | bytes 917504 | tf_op jit(solution)/shard_map/while/body/eval_jaxpr/all_to_all | solution.py:81
  108.1 13.8 %collective-permute-start.3 = (bf16[64,1024]{1,0:T(8,128)(2,1)S(1)}, bf16[64,1024]{1,0:T(8,128)(2,1)S(1)}, u32[]{:S(2)}, u32[]{:S(2)}) collective-permute-start(bf16[64,1024]{1,0:T(8,128)(2,1)S(1)} %maximum_select_fusion.9), channel_id=1, source_target_pairs={{0,4},{1,5},{2,6},{3,7},{4,0},{5,1},{6,2},{7,3},{8,12},{9,13},{10,... | collective-permute-start | bytes 393224 | tf_op jit(solution)/shard_map/while/body/eval_jaxpr/ppermute | solution.py:14
  151.2 18.7 %all-to-all-start.1 = ((bf16[32,2,3584]{2,1,0:T(2,128)(2,1)}), bf16[32,2,3584]{2,1,0:T(2,128)(2,1)S(1)}, u32[]{:S(2)}, u32[]{:S(2)}) async-start(bf16[32,2,3584]{2,1,0:T(2,128)(2,1)} %reshape.92), calls=%async_computation.1 | async-start | bytes 917504 | tf_op jit(solution)/shard_map/while/body/eval_jaxpr/all_to_all | solution.py:81
  165.1 15.1 %collective-permute-start.3 = (bf16[64,1024]{1,0:T(8,128)(2,1)S(1)}, bf16[64,1024]{1,0:T(8,128)(2,1)S(1)}, u32[]{:S(2)}, u32[]{:S(2)}) collective-permute-start(bf16[64,1024]{1,0:T(8,128)(2,1)S(1)} %maximum_select_fusion.9), channel_id=1, source_target_pairs={{0,4},{1,5},{2,6},{3,7},{4,0},{5,1},{6,2},{7,3},{8,12},{9,13},{10,... | collective-permute-start | bytes 393224 | tf_op jit(solution)/shard_map/while/body/eval_jaxpr/ppermute | solution.py:14
  171.5 11.6 %collective-permute-start = (bf16[32,3584]{1,0:T(8,128)(2,1)S(1)}, bf16[32,3584]{1,0:T(8,128)(2,1)S(1)}, u32[]{:S(2)}, u32[]{:S(2)}) collective-permute-start(bf16[32,3584]{1,0:T(8,128)(2,1)S(1)} %get-tuple-element.454), channel_id=1, source_target_pairs={{0,32},{32,64},{64,96},{96,128},{128,160},{160,192},{192,224},{1,3... | collective-permute-start | bytes 688136 | tf_op jit(solution)/shard_map/while/body/eval_jaxpr/ppermute | solution.py:20
  208.6 16.1 %all-to-all-start.1 = ((bf16[32,2,3584]{2,1,0:T(2,128)(2,1)}), bf16[32,2,3584]{2,1,0:T(2,128)(2,1)S(1)}, u32[]{:S(2)}, u32[]{:S(2)}) async-start(bf16[32,2,3584]{2,1,0:T(2,128)(2,1)} %reshape.92), calls=%async_computation.1 | async-start | bytes 917504 | tf_op jit(solution)/shard_map/while/body/eval_jaxpr/all_to_all | solution.py:81
  223.2 10.2 %collective-permute-start.3 = (bf16[64,1024]{1,0:T(8,128)(2,1)S(1)}, bf16[64,1024]{1,0:T(8,128)(2,1)S(1)}, u32[]{:S(2)}, u32[]{:S(2)}) collective-permute-start(bf16[64,1024]{1,0:T(8,128)(2,1)S(1)} %maximum_select_fusion.9), channel_id=1, source_target_pairs={{0,4},{1,5},{2,6},{3,7},{4,0},{5,1},{6,2},{7,3},{8,12},{9,13},{10,... | collective-permute-start | bytes 393224 | tf_op jit(solution)/shard_map/while/body/eval_jaxpr/ppermute | solution.py:14
  226.3 10.0 %collective-permute-start = (bf16[32,3584]{1,0:T(8,128)(2,1)S(1)}, bf16[32,3584]{1,0:T(8,128)(2,1)S(1)}, u32[]{:S(2)}, u32[]{:S(2)}) collective-permute-start(bf16[32,3584]{1,0:T(8,128)(2,1)S(1)} %get-tuple-element.454), channel_id=1, source_target_pairs={{0,32},{32,64},{64,96},{96,128},{128,160},{160,192},{192,224},{1,3... | collective-permute-start | bytes 688136 | tf_op jit(solution)/shard_map/while/body/eval_jaxpr/ppermute | solution.py:20
  263.8 16.2 %all-to-all-start.1 = ((bf16[32,2,3584]{2,1,0:T(2,128)(2,1)}), bf16[32,2,3584]{2,1,0:T(2,128)(2,1)S(1)}, u32[]{:S(2)}, u32[]{:S(2)}) async-start(bf16[32,2,3584]{2,1,0:T(2,128)(2,1)} %reshape.92), calls=%async_computation.1 | async-start | bytes 917504 | tf_op jit(solution)/shard_map/while/body/eval_jaxpr/all_to_all | solution.py:81
  277.3 11.3 %collective-permute-start.3 = (bf16[64,1024]{1,0:T(8,128)(2,1)S(1)}, bf16[64,1024]{1,0:T(8,128)(2,1)S(1)}, u32[]{:S(2)}, u32[]{:S(2)}) collective-permute-start(bf16[64,1024]{1,0:T(8,128)(2,1)S(1)} %maximum_select_fusion.9), channel_id=1, source_target_pairs={{0,4},{1,5},{2,6},{3,7},{4,0},{5,1},{6,2},{7,3},{8,12},{9,13},{10,... | collective-permute-start | bytes 393224 | tf_op jit(solution)/shard_map/while/body/eval_jaxpr/ppermute | solution.py:14
  319.0 16.3 %all-to-all-start.1 = ((bf16[32,2,3584]{2,1,0:T(2,128)(2,1)}), bf16[32,2,3584]{2,1,0:T(2,128)(2,1)S(1)}, u32[]{:S(2)}, u32[]{:S(2)}) async-start(bf16[32,2,3584]{2,1,0:T(2,128)(2,1)} %reshape.92), calls=%async_computation.1 | async-start | bytes 917504 | tf_op jit(solution)/shard_map/while/body/eval_jaxpr/all_to_all | solution.py:81
  332.1 11.7 %collective-permute-start.3 = (bf16[64,1024]{1,0:T(8,128)(2,1)S(1)}, bf16[64,1024]{1,0:T(8,128)(2,1)S(1)}, u32[]{:S(2)}, u32[]{:S(2)}) collective-permute-start(bf16[64,1024]{1,0:T(8,128)(2,1)S(1)} %maximum_select_fusion.9), channel_id=1, source_target_pairs={{0,4},{1,5},{2,6},{3,7},{4,0},{5,1},{6,2},{7,3},{8,12},{9,13},{10,... | collective-permute-start | bytes 393224 | tf_op jit(solution)/shard_map/while/body/eval_jaxpr/ppermute | solution.py:14
  374.2 16.2 %all-to-all-start.1 = ((bf16[32,2,3584]{2,1,0:T(2,128)(2,1)}), bf16[32,2,3584]{2,1,0:T(2,128)(2,1)S(1)}, u32[]{:S(2)}, u32[]{:S(2)}) async-start(bf16[32,2,3584]{2,1,0:T(2,128)(2,1)} %reshape.92), calls=%async_computation.1 | async-start | bytes 917504 | tf_op jit(solution)/shard_map/while/body/eval_jaxpr/all_to_all | solution.py:81
  387.4 11.6 %collective-permute-start.3 = (bf16[64,1024]{1,0:T(8,128)(2,1)S(1)}, bf16[64,1024]{1,0:T(8,128)(2,1)S(1)}, u32[]{:S(2)}, u32[]{:S(2)}) collective-permute-start(bf16[64,1024]{1,0:T(8,128)(2,1)S(1)} %maximum_select_fusion.9), channel_id=1, source_target_pairs={{0,4},{1,5},{2,6},{3,7},{4,0},{5,1},{6,2},{7,3},{8,12},{9,13},{10,... | collective-permute-start | bytes 393224 | tf_op jit(solution)/shard_map/while/body/eval_jaxpr/ppermute | solution.py:14
  429.4 16.3 %all-to-all-start.1 = ((bf16[32,2,3584]{2,1,0:T(2,128)(2,1)}), bf16[32,2,3584]{2,1,0:T(2,128)(2,1)S(1)}, u32[]{:S(2)}, u32[]{:S(2)}) async-start(bf16[32,2,3584]{2,1,0:T(2,128)(2,1)} %reshape.92), calls=%async_computation.1 | async-start | bytes 917504 | tf_op jit(solution)/shard_map/while/body/eval_jaxpr/all_to_all | solution.py:81
  442.5 11.7 %collective-permute-start.3 = (bf16[64,1024]{1,0:T(8,128)(2,1)S(1)}, bf16[64,1024]{1,0:T(8,128)(2,1)S(1)}, u32[]{:S(2)}, u32[]{:S(2)}) collective-permute-start(bf16[64,1024]{1,0:T(8,128)(2,1)S(1)} %maximum_select_fusion.9), channel_id=1, source_target_pairs={{0,4},{1,5},{2,6},{3,7},{4,0},{5,1},{6,2},{7,3},{8,12},{9,13},{10,... | collective-permute-start | bytes 393224 | tf_op jit(solution)/shard_map/while/body/eval_jaxpr/ppermute | solution.py:14
  484.6 16.2 %all-to-all-start.1 = ((bf16[32,2,3584]{2,1,0:T(2,128)(2,1)}), bf16[32,2,3584]{2,1,0:T(2,128)(2,1)S(1)}, u32[]{:S(2)}, u32[]{:S(2)}) async-start(bf16[32,2,3584]{2,1,0:T(2,128)(2,1)} %reshape.92), calls=%async_computation.1 | async-start | bytes 917504 | tf_op jit(solution)/shard_map/while/body/eval_jaxpr/all_to_all | solution.py:81
  497.8 11.6 %collective-permute-start.3 = (bf16[64,1024]{1,0:T(8,128)(2,1)S(1)}, bf16[64,1024]{1,0:T(8,128)(2,1)S(1)}, u32[]{:S(2)}, u32[]{:S(2)}) collective-permute-start(bf16[64,1024]{1,0:T(8,128)(2,1)S(1)} %maximum_select_fusion.9), channel_id=1, source_target_pairs={{0,4},{1,5},{2,6},{3,7},{4,0},{5,1},{6,2},{7,3},{8,12},{9,13},{10,... | collective-permute-start | bytes 393224 | tf_op jit(solution)/shard_map/while/body/eval_jaxpr/ppermute | solution.py:14
  539.8 16.3 %all-to-all-start.1 = ((bf16[32,2,3584]{2,1,0:T(2,128)(2,1)}), bf16[32,2,3584]{2,1,0:T(2,128)(2,1)S(1)}, u32[]{:S(2)}, u32[]{:S(2)}) async-start(bf16[32,2,3584]{2,1,0:T(2,128)(2,1)} %reshape.92), calls=%async_computation.1 | async-start | bytes 917504 | tf_op jit(solution)/shard_map/while/body/eval_jaxpr/all_to_all | solution.py:81
  552.9 11.7 %collective-permute-start.3 = (bf16[64,1024]{1,0:T(8,128)(2,1)S(1)}, bf16[64,1024]{1,0:T(8,128)(2,1)S(1)}, u32[]{:S(2)}, u32[]{:S(2)}) collective-permute-start(bf16[64,1024]{1,0:T(8,128)(2,1)S(1)} %maximum_select_fusion.9), channel_id=1, source_target_pairs={{0,4},{1,5},{2,6},{3,7},{4,0},{5,1},{6,2},{7,3},{8,12},{9,13},{10,... | collective-permute-start | bytes 393224 | tf_op jit(solution)/shard_map/while/body/eval_jaxpr/ppermute | solution.py:14
  595.0 16.2 %all-to-all-start.1 = ((bf16[32,2,3584]{2,1,0:T(2,128)(2,1)}), bf16[32,2,3584]{2,1,0:T(2,128)(2,1)S(1)}, u32[]{:S(2)}, u32[]{:S(2)}) async-start(bf16[32,2,3584]{2,1,0:T(2,128)(2,1)} %reshape.92), calls=%async_computation.1 | async-start | bytes 917504 | tf_op jit(solution)/shard_map/while/body/eval_jaxpr/all_to_all | solution.py:81
  608.2 11.6 %collective-permute-start.3 = (bf16[64,1024]{1,0:T(8,128)(2,1)S(1)}, bf16[64,1024]{1,0:T(8,128)(2,1)S(1)}, u32[]{:S(2)}, u32[]{:S(2)}) collective-permute-start(bf16[64,1024]{1,0:T(8,128)(2,1)S(1)} %maximum_select_fusion.9), channel_id=1, source_target_pairs={{0,4},{1,5},{2,6},{3,7},{4,0},{5,1},{6,2},{7,3},{8,12},{9,13},{10,... | collective-permute-start | bytes 393224 | tf_op jit(solution)/shard_map/while/body/eval_jaxpr/ppermute | solution.py:14
  (53 other events, 233.6 us)
where the time goes:
time: 628 us; the launch traced here: 624 us
  blocking collectives  222 us (35%)
  starting transfers between devices  183 us (29%)
  waiting for transfers between devices  88 us (14%)
  matrix products  47.3 us (8%)
  local copies, waits for them, and re-layouts  44.6 us (7%)
  other arithmetic  37.4 us (6%)
    all_to_all x11, blocking collectives, layer_step(): lax.all_to_all(outbound, 'expert', split_axis=0, concat_axis=0, tiled=True)  222 us
    ppermute x11, starting transfers between devices, passed_along(): return lax.ppermute(value, axis, pairs)  76.2 us
    ppermute x33, starting transfers between devices, partner(): lax.ppermute(value, axis, [(i, i ^ 1 << bit) for i in range(lax.axis_size...  61.6 us
    all_to_all x11, starting transfers between devices, layer_step(): lax.all_to_all(partial_value.reshape(devices, CAP, width), 'expert', spli...  45 us
    ppermute x33, waiting for transfers between devices, partner(): lax.ppermute(value, axis, [(i, i ^ 1 << bit) for i in range(lax.axis_size...  42.1 us
    ppermute x11, waiting for transfers between devices, passed_along(): return lax.ppermute(value, axis, pairs)  25.1 us
    dot_general x11, matrix products, layer_step(): gate_act = jnp.dot(rows, gate_weight, preferred_element_type=jnp.float32)  23 us
    all_to_all x11, waiting for transfers between devices, layer_step(): lax.all_to_all(partial_value.reshape(devices, CAP, width), 'expert', spli...  20.8 us
  transfers between devices with their start and end apart: 55, of which 44 were waited for; matrix products, arithmetic and copies ran while one was open for 7% of the time, Pallas kernels for 0%

commit v1 on v0

v1 whole, which is shorter than its diff:
```python
import functools

import jax
import jax.numpy as jnp
from jax import lax
from jax.experimental import pallas as pl
from jax.experimental.pallas import tpu as pltpu
from jax.sharding import PartitionSpec as P

GROUP = 8
CAP = 2
EPSILON = 1e-06
MESH = pl.DeviceIdType.MESH
PLANES = 8
RING = 4
BF16 = jnp.bfloat16
F32 = jnp.float32


def first_and_second(route, expert, lanes):
    routed = jnp.max((route == expert).astype(F32), axis=0, keepdims=True)
    first = jnp.min(jnp.where(routed > 0, lanes, 1000), axis=1, keepdims=True)
    slot0 = jnp.where(lanes == first, routed, 0.0)
    return slot0, routed - slot0


def kernel(
    stream, gain, wg, wu, wd, routes, gates,
    out, hess,
    wg_v, wu_v, wd_v, routes_next,
    pick_own, mix_full, mix_next,
    xin, xout, sbuf, abuf, arecv, rows, part, drecv, ebuf, erecv, hid, gram,
    w_sem, in_sem, out_sem, hess_sem,
    r_send, r_recv, s_send, a_send, a_recv, b_send, b_recv,
    h_send, h_recv, d_send, d_recv, e_send, e_recv, x_send, x_recv,
):
    fronts, tokens, width = xin.shape
    flight = PLANES // 2
    sections = lax.axis_size("layer")
    layer = lax.axis_index("layer")
    place = lax.axis_index("expert")
    z, x = place // RING, place % RING
    half = z % 2
    member = half * RING + x
    is_first, is_last = layer == 0, layer == sections - 1

    def at_z(step):
        return lax.rem(z + step, PLANES)

    def at_x(step):
        return lax.rem(x + step, RING)

    def peers():
        group = []
        for other in (0, 1):
            for step in range(RING):
                if other or step:
                    p = lax.rem(half + other, 2)
                    nx = at_x(step)
                    group.append(((z - half + p) * RING + nx, p * RING + nx))
        return group

    group = peers()

    def remote(src, dst, send, recv, to_layer, to_place):
        return pltpu.make_async_remote_copy(
            src_ref=src, dst_ref=dst, send_sem=send, recv_sem=recv,
            device_id=(to_layer, to_place), device_id_type=MESH,
        )

    def copy_routes(to_layer):
        return remote(routes, routes_next, r_send, r_recv, to_layer, place)

    def copy_s(f, to_z):
        return remote(sbuf.at[f, to_z // 2], arecv.at[f, z], s_send.at[f, to_z], a_recv.at[f, z],
                      layer, to_z * RING + x)

    def copy_a(f, to_z, slot, to_layer):
        return remote(abuf.at[f, to_z // 2], arecv.at[f, slot], a_send.at[f, to_z], a_recv.at[f, slot],
                      to_layer, to_z * RING + x)

    def copy_b(f, to_x, slot):
        return remote(rows.at[f, slot], rows.at[f, slot], b_send.at[f, to_x], b_recv.at[f, slot],
                      layer, z * RING + to_x)

    def copy_h(f, to_place, to_member, slot):
        return remote(hid.at[slot, f], hid.at[slot, f], h_send.at[f, to_member], h_recv.at[f, slot],
                      layer, to_place)

    def copy_d(f, to_x, slot):
        return remote(part.at[f, to_x], drecv.at[f, slot], d_send.at[f, to_x], d_recv.at[f, slot],
                      layer, z * RING + to_x)

    def copy_e(f, to_z, slot):
        return remote(ebuf.at[f, to_z], erecv.at[f, slot], e_send.at[f, to_z], e_recv.at[f, slot],
                      layer, to_z * RING + x)

    def copy_x(f, to_layer):
        return remote(xout.at[f], xin.at[f], x_send.at[f], x_recv.at[f], to_layer, place)

    def load_stream(f):
        return pltpu.make_async_copy(stream.at[f], xin.at[f], in_sem.at[f])

    def store_out(f):
        return pltpu.make_async_copy(xout.at[f], out.at[0, f], out_sem.at[f])

    weights = (
        pltpu.make_async_copy(wg.at[0], wg_v, w_sem.at[0]),
        pltpu.make_async_copy(wu.at[0], wu_v, w_sem.at[1]),
        pltpu.make_async_copy(wd.at[0], wd_v, w_sem.at[2]),
    )

    @pl.when(is_first)
    def _():
        for f in range(fronts):
            load_stream(f).start()

    for load in weights:
        load.start()

    barrier = pltpu.get_barrier_semaphore()

    def greet(to_layer, to_place):
        pl.semaphore_signal(barrier, inc=1, device_id=(to_layer, to_place), device_id_type=MESH)

    @pl.when(layer > 0)
    def _():
        for step in range(PLANES):
            greet(layer - 1, at_z(step) * RING + x)

    @pl.when(layer < sections - 1)
    def _():
        greet(layer + 1, place)

    for step in range(1, PLANES):
        greet(layer, at_z(step) * RING + x)
    for step in range(1, RING):
        greet(layer, z * RING + at_x(step))
    for step in range(1, RING):
        greet(layer, (z - half + (1 - half)) * RING + at_x(step))

    lanes = lax.broadcasted_iota(jnp.int32, (1, tokens), 1)
    row8 = lax.broadcasted_iota(jnp.int32, (flight * CAP, tokens), 0)
    row16 = lax.broadcasted_iota(jnp.int32, (2 * flight * CAP, tokens), 0)
    eye = (
        lax.broadcasted_iota(jnp.int32, (tokens, tokens), 0)
        == lax.broadcasted_iota(jnp.int32, (tokens, tokens), 1)
    ).astype(BF16)

    def own_tables(f):
        route, gate = routes[f], gates[f]
        pick = jnp.zeros((flight * CAP, tokens), F32)
        scaled = jnp.zeros((2 * flight * CAP, tokens), F32)
        for expert in range(flight):
            slots = first_and_second(route, expert, lanes)
            weight = jnp.sum(jnp.where(route == expert, gate, 0.0), axis=0, keepdims=True)
            for c in range(CAP):
                pick = jnp.where(row8 == expert * CAP + c, slots[c], pick)
                here = jnp.logical_and(row16 // (2 * CAP) == expert, row16 % CAP == c)
                scaled = jnp.where(here, slots[c] * weight, scaled)
        pick_own[f] = pick.astype(BF16)
        mix = scaled.T
        high = mix.astype(BF16)
        low = (mix - high.astype(F32)).astype(BF16)
        mix_full[f] = jnp.concatenate([eye, high, low], axis=1)

    def next_tables(f):
        route = routes_next[f]
        pick = jnp.zeros((flight * CAP, tokens), F32)
        for expert in range(flight):
            slots = first_and_second(route, expert, lanes)
            for c in range(CAP):
                pick = jnp.where(row8 == expert * CAP + c, slots[c], pick)
        mix_next[f] = jnp.dot(
            pick.astype(BF16), mix_full[f], preferred_element_type=F32
        ).astype(BF16)

    for f in range(fronts):
        own_tables(f)

    @pl.when(jnp.logical_and(is_first, is_last))
    def _():
        pl.semaphore_wait(barrier, 13)

    @pl.when(jnp.logical_and(is_first, jnp.logical_not(is_last)))
    def _():
        pl.semaphore_wait(barrier, 13 + PLANES)

    @pl.when(jnp.logical_and(jnp.logical_not(is_first), is_last))
    def _():
        pl.semaphore_wait(barrier, 13 + 1)

    @pl.when(jnp.logical_and(jnp.logical_not(is_first), jnp.logical_not(is_last)))
    def _():
        pl.semaphore_wait(barrier, 13 + 1 + PLANES)

    @pl.when(layer > 0)
    def _():
        copy_routes(layer - 1).start()

    def stage_s(f):
        load_stream(f).wait()
        picked = jnp.dot(pick_own[f], xin[f], preferred_element_type=F32).astype(BF16)
        sbuf[f] = picked.reshape(flight, CAP, width)
        for step in range(1, PLANES):
            copy_s(f, at_z(step)).start()
        arecv[f, z] = sbuf[f, z // 2]

    def stage_a(f):
        for step in range(1, PLANES):
            copy_a(f, z, at_z(step), layer).wait_recv()

        @pl.when(layer > 0)
        def _():
            copy_a(f, z, z, layer).wait_recv()

        wide = arecv[f].reshape(PLANES * CAP, width).astype(F32)
        scale = lax.rsqrt(jnp.mean(wide * wide, axis=-1, keepdims=True) + EPSILON)
        rows[f, x] = (wide * scale * gain[...]).astype(BF16)
        for step in (2, 1, 3):
            copy_b(f, at_x(step), x).start()

    def stage_b(f):
        for step in range(1, RING):
            copy_b(f, x, at_x(step)).wait_recv()
        all_rows = rows[f].reshape(RING * PLANES * CAP, width)
        gate_act = jnp.dot(all_rows, wg_v[...], preferred_element_type=F32)
        up_act = jnp.dot(all_rows, wu_v[...], preferred_element_type=F32)
        hidden = (jax.nn.silu(gate_act) * up_act).astype(BF16)
        partial = jnp.dot(hidden, wd_v[...], preferred_element_type=F32).astype(BF16)
        part[f] = partial.reshape(RING, PLANES * CAP, width)
        for step in (2, 1, 3):
            copy_d(f, at_x(step), x).start()
        hid[member, f] = hidden
        for to_place, to_member in group:
            copy_h(f, to_place, to_member, member).start()

    def stage_d(f):
        for step in range(1, RING):
            copy_d(f, x, at_x(step)).wait_recv()
        total = part[f, x].astype(F32)
        for step in range(1, RING):
            total = total + drecv[f, at_x(step)].astype(F32)
        ebuf[f] = total.astype(BF16).reshape(PLANES, CAP, width)
        for step in range(1, PLANES):
            copy_e(f, at_z(step), z).start()
        erecv[f, z] = ebuf[f, z]

    def stage_e(f):
        @pl.when(layer > 0)
        def _():
            copy_x(f, layer).wait_recv()

        for step in range(1, PLANES):
            copy_e(f, z, at_z(step)).wait_recv()
        returned = erecv[f].reshape(PLANES * CAP, width)
        stack = jnp.concatenate([xin[f], returned, returned], axis=0)

        @pl.when(layer < sections - 1)
        def _():
            picked = jnp.dot(mix_next[f], stack, preferred_element_type=F32).astype(BF16)
            abuf[f] = picked.reshape(flight, CAP, width)
            for step in range(PLANES):
                copy_a(f, at_z(step), z, layer + 1).start()

        xout[f] = jnp.dot(mix_full[f], stack, preferred_element_type=F32).astype(BF16)

        @pl.when(layer < sections - 1)
        def _():
            copy_x(f, layer + 1).start()

        store_out(f).start()

    @pl.when(is_first)
    def _():
        stage_s(0)

    @pl.when(layer < sections - 1)
    def _():
        copy_routes(layer).wait_recv()
        for f in range(fronts):
            next_tables(f)

    for load in weights:
        load.wait()

    stage_a(0)

    @pl.when(is_first)
    def _():
        stage_s(1)

    stage_b(0)

    @pl.when(is_first)
    def _():
        for f in range(2, fronts):
            stage_s(f)

    def steady(f, carry):
        stage_d(f)
        stage_a(f + 1)
        stage_e(f)
        stage_b(f + 1)
        return carry

    lax.fori_loop(0, fronts - 1, steady, 0)
    stage_d(fronts - 1)

    for f in range(fronts):
        for _, slot in group:
            copy_h(f, place, member, slot).wait_recv()
    mine = hid[member].reshape(-1, hid.shape[-1])
    units = hid.shape[-1]
    for slot in range(GROUP):
        theirs = hid[slot].reshape(-1, units)
        gram[:, slot * units:(slot + 1) * units] = lax.dot_general(
            mine, theirs, (((0,), (0,)), ((), ())), preferred_element_type=F32
        ) * (1.0 / (fronts * CAP))
    store_gram = pltpu.make_async_copy(gram, hess.at[0], hess_sem)
    store_gram.start()

    stage_e(fronts - 1)

    @pl.when(layer > 0)
    def _():
        copy_routes(layer - 1).wait_send()

    def finish(f, carry):
        for step in range(1, RING):
            copy_b(f, at_x(step), x).wait_send()
            copy_d(f, at_x(step), x).wait_send()
        for to_place, to_member in group:
            copy_h(f, to_place, to_member, member).wait_send()
        for step in range(1, PLANES):
            copy_e(f, at_z(step), z).wait_send()

        @pl.when(is_first)
        def _():
            for step in range(1, PLANES):
                copy_s(f, at_z(step)).wait_send()

        @pl.when(layer < sections - 1)
        def _():
            for step in range(PLANES):
                copy_a(f, at_z(step), z, layer + 1).wait_send()
            copy_x(f, layer + 1).wait_send()

        store_out(f).wait()
        return carry

    lax.fori_loop(0, fronts, finish, 0)
    store_gram.wait()


def shards(stream_in, gain, w_gate, w_up, w_down, routes, gates):
    fronts, tokens, width = stream_in.shape
    units = w_gate.shape[2]
    slots = PLANES * CAP
    flight = PLANES // 2
    dma = pltpu.SemaphoreType.DMA
    anywhere = pl.BlockSpec(memory_space=pl.ANY)
    vmem = pl.BlockSpec(memory_space=pltpu.VMEM)
    route_cols = jnp.swapaxes(routes[0], 1, 2)
    gate_cols = jnp.swapaxes(gates[0], 1, 2)
    return pl.pallas_call(
        kernel,
        out_shape=(
            jax.ShapeDtypeStruct((1, fronts, tokens, width), BF16),
            jax.ShapeDtypeStruct((1, units, GROUP * units), F32),
        ),
        in_specs=[anywhere, vmem, anywhere, anywhere, anywhere, vmem, vmem],
        out_specs=(anywhere, anywhere),
        scratch_shapes=[
            pltpu.VMEM((width, units), BF16),
            pltpu.VMEM((width, units), BF16),
            pltpu.VMEM((units, width), BF16),
            pltpu.VMEM(route_cols.shape, jnp.int32),
            pltpu.VMEM((fronts, flight * CAP, tokens), BF16),
            pltpu.VMEM((fronts, tokens, tokens + 2 * slots), BF16),
            pltpu.VMEM((fronts, flight * CAP, tokens + 2 * slots), BF16),
            pltpu.VMEM((fronts, tokens, width), BF16),
            pltpu.VMEM((fronts, tokens, width), BF16),
            pltpu.VMEM((fronts, flight, CAP, width), BF16),
            pltpu.VMEM((fronts, flight, CAP, width), BF16),
            pltpu.VMEM((fronts, PLANES, CAP, width), BF16),
            pltpu.VMEM((fronts, RING, slots, width), BF16),
            pltpu.VMEM((fronts, RING, slots, width), BF16),
            pltpu.VMEM((fronts, RING, slots, width), BF16),
            pltpu.VMEM((fronts, PLANES, CAP, width), BF16),
            pltpu.VMEM((fronts, PLANES, CAP, width), BF16),
            pltpu.VMEM((GROUP, fronts, RING * slots, units), BF16),
            pltpu.VMEM((units, GROUP * units), F32),
            dma((3,)), dma((fronts,)), dma((fronts,)), dma,
            dma, dma,
            dma((fronts, PLANES)),
            dma((fronts, PLANES)), dma((fronts, PLANES)),
            dma((fronts, RING)), dma((fronts, RING)),
            dma((fronts, GROUP)), dma((fronts, GROUP)),
            dma((fronts, RING)), dma((fronts, RING)),
            dma((fronts, PLANES)), dma((fronts, PLANES)),
            dma((fronts,)), dma((fronts,)),
        ],
        compiler_params=pltpu.CompilerParams(
            collective_id=0, has_side_effects=True, vmem_limit_bytes=48 * 1024 * 1024
        ),
    )(stream_in, gain, w_gate, w_up, w_down, route_cols, gate_cols)


def solution(mesh):
    return jax.shard_map(
        shards,
        mesh=mesh,
        in_specs=(
            P(None, "expert", None),
            P("layer", None),
            P("layer", None, "expert"),
            P("layer", None, "expert"),
            P("layer", "expert", None),
            P("layer", None, "expert", None),
            P("layer", None, "expert", None),
        ),
        out_specs=(P("layer", None, "expert", None), P("layer", "expert", None)),
        check_vma=False,
    )
```

time: 628 us -> 274 us (0.44)
  the two profiles are of different devices: /device:TPU:1 before, /device:TPU:25 now
where the time goes in v1:
time: 274 us
  Pallas kernels  263 us (96%)
  local copies, waits for them, and re-layouts  10.4 us (4%)
    pallas_call x1, Pallas kernels, shards(): pl.pallas_call(kernel, out_shape=(jax.ShapeDtypeStruct((1, fronts, tokens...  263 us
    unnamed x14, local copies, waits for them, and re-layouts  10.4 us

profile of v1, /device:TPU:25, one launch (start us, length us, event | category | flops | bytes accessed | tf_op | source)
XLA Modules:
  0.0 274.0 jit_solution(15827383948839629278)
XLA Ops:
  0.6 0.0 copy-start
  0.6 1.5 copy-done
  2.1 0.0 copy-start.1
  2.1 1.5 copy-done.1
  3.6 0.0 copy-start.2
  3.6 1.2 copy-done.2
  4.8 0.0 copy-start.3
  4.8 0.7 copy-done.3
  5.5 0.0 copy-start.4
  5.5 0.7 copy-done.4
  6.2 0.0 copy-start.5
  6.2 0.7 copy-done.5
  7.0 263.0 %shard_map.86 = (bf16[1,4,32,3584]{3,2,1,0:T(8,128)(2,1)S(1)}, f32[1,256,2048]{2,1,0:T(8,128)}) custom-call(bf16[4,32,3584]{2,1,0:T(8,128)(2,1)S(1)} %copy-done.2, f32[1,3584]{1,0:T(1,128)S(1)} %copy-done.5, bf16[1,3584,256]{2,1,0:T(8,128)(2,1)S(1)} %copy-done, bf16[1,3584,256]{2,1,0:T(8,128)(2,1)S(1)} %copy-done.1, bf16[1,256,3584]{2,1,0:T(8,128)(2,1)} %wd.1, ...), custom_call_target="tpu_custom_call" | custom-call | tf_op jit(solution)/shard_map/pallas_call | solution.py:366
  270.0 0.9 copy.11
  270.9 3.1 %copy.12 = f32[1,256,2048]{2,1,0:T(8,128)} copy(f32[1,256,2048]{2,1,0:T(8,128)} %get-tuple-element.5) | data formatting | bytes 4194304
Async XLA Ops:
  0.6 1.5 copy-start
  2.1 1.5 copy-start.1
  3.6 1.2 copy-start.2
  4.8 0.7 copy-start.3
  5.5 0.7 copy-start.4
  6.2 0.7 copy-start.5

commit v2 on v1

--- a/solution.py
+++ b/solution.py
@@ -13,6 +13,7 @@
 MESH = pl.DeviceIdType.MESH
 PLANES = 8
 RING = 4
+CHUNKS = 4
 BF16 = jnp.bfloat16
 F32 = jnp.float32
 
@@ -29,12 +30,13 @@
     out, hess,
     wg_v, wu_v, wd_v, routes_next,
     pick_own, mix_full, mix_next,
-    xin, xout, sbuf, abuf, arecv, rows, part, drecv, ebuf, erecv, hid, gram,
+    xin, xout, sbuf, abuf, arecv, scales, rows, part, drecv, ebuf, erecv, hid, gram,
     w_sem, in_sem, out_sem, hess_sem,
-    r_send, r_recv, s_send, a_send, a_recv, b_send, b_recv,
+    r_send, r_recv, s_send, a_send, a_recv, b_send, b_recv, c_send, c_recv,
     h_send, h_recv, d_send, d_recv, e_send, e_recv, x_send, x_recv,
 ):
     fronts, tokens, width = xin.shape
+    chunks, part_width = sbuf.shape[1], sbuf.shape[-1]
     flight = PLANES // 2
     sections = lax.axis_size("layer")
     layer = lax.axis_index("layer")
@@ -71,29 +73,36 @@
     def copy_routes(to_layer):
         return remote(routes, routes_next, r_send, r_recv, to_layer, place)
 
-    def copy_s(f, to_z):
-        return remote(sbuf.at[f, to_z // 2], arecv.at[f, z], s_send.at[f, to_z], a_recv.at[f, z],
-                      layer, to_z * RING + x)
-
-    def copy_a(f, to_z, slot, to_layer):
-        return remote(abuf.at[f, to_z // 2], arecv.at[f, slot], a_send.at[f, to_z], a_recv.at[f, slot],
-                      to_layer, to_z * RING + x)
-
-    def copy_b(f, to_x, slot):
-        return remote(rows.at[f, slot], rows.at[f, slot], b_send.at[f, to_x], b_recv.at[f, slot],
-                      layer, z * RING + to_x)
+    def copy_s(f, c, to_z):
+        return remote(sbuf.at[f, c, to_z // 2], arecv.at[f, c, z],
+                      s_send.at[f, c, to_z], a_recv.at[f, c, z], layer, to_z * RING + x)
+
+    def copy_a(f, c, to_z, slot, to_layer):
+        return remote(abuf.at[f, c, to_z // 2], arecv.at[f, c, slot],
+                      a_send.at[f, c, to_z], a_recv.at[f, c, slot], to_layer, to_z * RING + x)
+
+    def copy_b(f, c, to_x, slot):
+        return remote(rows.at[f, c, slot], rows.at[f, c, slot],
+                      b_send.at[f, c, to_x], b_recv.at[f, c, slot], layer, z * RING + to_x)
+
+    def copy_c(f, to_x, slot):
+        return remote(scales.at[f, slot], scales.at[f, slot],
+                      c_send.at[f, to_x], c_recv.at[f, slot], layer, z * RING + to_x)
 
     def copy_h(f, to_place, to_member, slot):
         return remote(hid.at[slot, f], hid.at[slot, f], h_send.at[f, to_member], h_recv.at[f, slot],
                       layer, to_place)
 
-    def copy_d(f, to_x, slot):
-        return remote(part.at[f, to_x], drecv.at[f, slot], d_send.at[f, to_x], d_recv.at[f, slot],
-                      layer, z * RING + to_x)
-
-    def copy_e(f, to_z, slot):
-        return remote(ebuf.at[f, to_z], erecv.at[f, slot], e_send.at[f, to_z], e_recv.at[f, slot],
-                      layer, to_z * RING + x)
+    def copy_d(f, c, to_x, slot):
+        return remote(part.at[f, c, to_x], drecv.at[f, c, slot],
+                      d_send.at[f, c, to_x], d_recv.at[f, c, slot], layer, z * RING + to_x)
+
+    def copy_e(f, c, to_z, slot):
+        return remote(ebuf.at[f, c, to_z], erecv.at[f, c, slot],
+                      e_send.at[f, c, to_z], e_recv.at[f, c, slot], layer, to_z * RING + x)
+
+    def columns(c):
+        return slice(c * part_width, (c + 1) * part_width)
 
     def copy_x(f, to_layer):
         return remote(xout.at[f], xin.at[f], x_send.at[f], x_recv.at[f], to_layer, place)
@@ -200,70 +209,92 @@
 
     def stage_s(f):
         load_stream(f).wait()
-        picked = jnp.dot(pick_own[f], xin[f], preferred_element_type=F32).astype(BF16)
-        sbuf[f] = picked.reshape(flight, CAP, width)
-        for step in range(1, PLANES):
-            copy_s(f, at_z(step)).start()
-        arecv[f, z] = sbuf[f, z // 2]
+        for c in range(chunks):
+            picked = jnp.dot(pick_own[f], xin[f, :, columns(c)], preferred_element_type=F32)
+            sbuf[f, c] = picked.astype(BF16).reshape(flight, CAP, part_width)
+            for step in range(1, PLANES):
+                copy_s(f, c, at_z(step)).start()
+            arecv[f, c, z] = sbuf[f, c, z // 2]
 
     def stage_a(f):
-        for step in range(1, PLANES):
-            copy_a(f, z, at_z(step), layer).wait_recv()
-
-        @pl.when(layer > 0)
-        def _():
-            copy_a(f, z, z, layer).wait_recv()
-
-        wide = arecv[f].reshape(PLANES * CAP, width).astype(F32)
-        scale = lax.rsqrt(jnp.mean(wide * wide, axis=-1, keepdims=True) + EPSILON)
-        rows[f, x] = (wide * scale * gain[...]).astype(BF16)
+        squares = jnp.zeros((PLANES * CAP, 1), F32)
+        for c in range(chunks):
+            for step in range(1, PLANES):
+                copy_a(f, c, z, at_z(step), layer).wait_recv()
+
+            @pl.when(layer > 0)
+            def _():
+                copy_a(f, c, z, z, layer).wait_recv()
+
+            wide = arecv[f, c].reshape(PLANES * CAP, part_width).astype(F32)
+            rows[f, c, x] = (wide * gain[:, columns(c)]).astype(BF16)
+            for step in (2, 1, 3):
+                copy_b(f, c, at_x(step), x).start()
+            squares = squares + jnp.sum(wide * wide, axis=-1, keepdims=True)
+        scale = lax.rsqrt(squares * (1.0 / width) + EPSILON)
+        scales[f, x] = jnp.broadcast_to(scale, scales.shape[2:])
         for step in (2, 1, 3):
-            copy_b(f, at_x(step), x).start()
+            copy_c(f, at_x(step), x).start()
 
     def stage_b(f):
+        count = RING * PLANES * CAP
+        gate_act = jnp.zeros((count, wg_v.shape[1]), F32)
+        up_act = jnp.zeros((count, wg_v.shape[1]), F32)
+        for c in range(chunks):
+            for step in range(1, RING):
+                copy_b(f, c, x, at_x(step)).wait_recv()
+            all_rows = rows[f, c].reshape(count, part_width)
+            gate_act += jnp.dot(all_rows, wg_v[columns(c), :], preferred_element_type=F32)
+            up_act += jnp.dot(all_rows, wu_v[columns(c), :], preferred_element_type=F32)
         for step in range(1, RING):
-            copy_b(f, x, at_x(step)).wait_recv()
-        all_rows = rows[f].reshape(RING * PLANES * CAP, width)
-        gate_act = jnp.dot(all_rows, wg_v[...], preferred_element_type=F32)
-        up_act = jnp.dot(all_rows, wu_v[...], preferred_element_type=F32)
-        hidden = (jax.nn.silu(gate_act) * up_act).astype(BF16)
-        partial = jnp.dot(hidden, wd_v[...], preferred_element_type=F32).astype(BF16)
-        part[f] = partial.reshape(RING, PLANES * CAP, width)
-        for step in (2, 1, 3):
-            copy_d(f, at_x(step), x).start()
+            copy_c(f, x, at_x(step)).wait_recv()
+        scale = scales[f].reshape(count, scales.shape[-1])[:, :1]
+        hidden = (jax.nn.silu(gate_act * scale) * (up_act * scale)).astype(BF16)
+        for c in range(chunks):
+            partial = jnp.dot(hidden, wd_v[:, columns(c)], preferred_element_type=F32)
+            part[f, c] = partial.astype(BF16).reshape(RING, PLANES * CAP, part_width)
+            for step in (2, 1, 3):
+                copy_d(f, c, at_x(step), x).start()
         hid[member, f] = hidden
         for to_place, to_member in group:
             copy_h(f, to_place, to_member, member).start()
 
     def stage_d(f):
-        for step in range(1, RING):
-            copy_d(f, x, at_x(step)).wait_recv()
-        total = part[f, x].astype(F32)
-        for step in range(1, RING):
-            total = total + drecv[f, at_x(step)].astype(F32)
-        ebuf[f] = total.astype(BF16).reshape(PLANES, CAP, width)
-        for step in range(1, PLANES):
-            copy_e(f, at_z(step), z).start()
-        erecv[f, z] = ebuf[f, z]
+        for c in range(chunks):
+            for step in range(1, RING):
+                copy_d(f, c, x, at_x(step)).wait_recv()
+            total = part[f, c, x].astype(F32)
+            for step in range(1, RING):
+                total = total + drecv[f, c, at_x(step)].astype(F32)
+            ebuf[f, c] = total.astype(BF16).reshape(PLANES, CAP, part_width)
+            for step in range(1, PLANES):
+                copy_e(f, c, at_z(step), z).start()
+            erecv[f, c, z] = ebuf[f, c, z]
 
     def stage_e(f):
         @pl.when(layer > 0)
         def _():
             copy_x(f, layer).wait_recv()
 
-        for step in range(1, PLANES):
-            copy_e(f, z, at_z(step)).wait_recv()
-        returned = erecv[f].reshape(PLANES * CAP, width)
-        stack = jnp.concatenate([xin[f], returned, returned], axis=0)
-
-        @pl.when(layer < sections - 1)
-        def _():
-            picked = jnp.dot(mix_next[f], stack, preferred_element_type=F32).astype(BF16)
-            abuf[f] = picked.reshape(flight, CAP, width)
-            for step in range(PLANES):
-                copy_a(f, at_z(step), z, layer + 1).start()
-
-        xout[f] = jnp.dot(mix_full[f], stack, preferred_element_type=F32).astype(BF16)
+        def stack(c):
+            returned = erecv[f, c].reshape(PLANES * CAP, part_width)
+            return jnp.concatenate([xin[f, :, columns(c)], returned, returned], axis=0)
+
+        for c in range(chunks):
+            for step in range(1, PLANES):
+                copy_e(f, c, z, at_z(step)).wait_recv()
+
+            @pl.when(layer < sections - 1)
+            def _():
+                picked = jnp.dot(mix_next[f], stack(c), preferred_element_type=F32)
+                abuf[f, c] = picked.astype(BF16).reshape(flight, CAP, part_width)
+                for step in range(PLANES):
+                    copy_a(f, c, at_z(step), z, layer + 1).start()
+
+        for c in range(chunks):
+            xout[f, :, columns(c)] = jnp.dot(
+                mix_full[f], stack(c), preferred_element_type=F32
+            ).astype(BF16)
 
         @pl.when(layer < sections - 1)
         def _():
@@ -286,18 +317,14 @@
 
     stage_a(0)
 
-    @pl.when(is_first)
-    def _():
-        stage_s(1)
-
     stage_b(0)
 
-    @pl.when(is_first)
-    def _():
-        for f in range(2, fronts):
-            stage_s(f)
-
     def steady(f, carry):
+
+        @pl.when(is_first)
+        def _():
+            stage_s(f + 1)
+
         stage_d(f)
         stage_a(f + 1)
         stage_e(f)
@@ -328,22 +355,27 @@
 
     def finish(f, carry):
         for step in range(1, RING):
-            copy_b(f, at_x(step), x).wait_send()
-            copy_d(f, at_x(step), x).wait_send()
+            copy_c(f, at_x(step), x).wait_send()
         for to_place, to_member in group:
             copy_h(f, to_place, to_member, member).wait_send()
-        for step in range(1, PLANES):
-            copy_e(f, at_z(step), z).wait_send()
+        for c in range(chunks):
+            for step in range(1, RING):
+                copy_b(f, c, at_x(step), x).wait_send()
+                copy_d(f, c, at_x(step), x).wait_send()
+            for step in range(1, PLANES):
+                copy_e(f, c, at_z(step), z).wait_send()
 
         @pl.when(is_first)
         def _():
-            for step in range(1, PLANES):
-                copy_s(f, at_z(step)).wait_send()
+            for c in range(chunks):
+                for step in range(1, PLANES):
+                    copy_s(f, c, at_z(step)).wait_send()
 
         @pl.when(layer < sections - 1)
         def _():
-            for step in range(PLANES):
-                copy_a(f, at_z(step), z, layer + 1).wait_send()
+            for c in range(chunks):
+                for step in range(PLANES):
+                    copy_a(f, c, at_z(step), z, layer + 1).wait_send()
             copy_x(f, layer + 1).wait_send()
 
         store_out(f).wait()
@@ -358,6 +390,7 @@
     units = w_gate.shape[2]
     slots = PLANES * CAP
     flight = PLANES // 2
+    part_width = width // CHUNKS
     dma = pltpu.SemaphoreType.DMA
     anywhere = pl.BlockSpec(memory_space=pl.ANY)
     vmem = pl.BlockSpec(memory_space=pltpu.VMEM)
@@ -381,28 +414,30 @@
             pltpu.VMEM((fronts, flight * CAP, tokens + 2 * slots), BF16),
             pltpu.VMEM((fronts, tokens, width), BF16),
             pltpu.VMEM((fronts, tokens, width), BF16),
-            pltpu.VMEM((fronts, flight, CAP, width), BF16),
-            pltpu.VMEM((fronts, flight, CAP, width), BF16),
-            pltpu.VMEM((fronts, PLANES, CAP, width), BF16),
-            pltpu.VMEM((fronts, RING, slots, width), BF16),
-            pltpu.VMEM((fronts, RING, slots, width), BF16),
-            pltpu.VMEM((fronts, RING, slots, width), BF16),
-            pltpu.VMEM((fronts, PLANES, CAP, width), BF16),
-            pltpu.VMEM((fronts, PLANES, CAP, width), BF16),
+            pltpu.VMEM((fronts, CHUNKS, flight, CAP, part_width), BF16),
+            pltpu.VMEM((fronts, CHUNKS, flight, CAP, part_width), BF16),
+            pltpu.VMEM((fronts, CHUNKS, PLANES, CAP, part_width), BF16),
+            pltpu.VMEM((fronts, RING, slots, 128), F32),
+            pltpu.VMEM((fronts, CHUNKS, RING, slots, part_width), BF16),
+            pltpu.VMEM((fronts, CHUNKS, RING, slots, part_width), BF16),
+            pltpu.VMEM((fronts, CHUNKS, RING, slots, part_width), BF16),
+            pltpu.VMEM((fronts, CHUNKS, PLANES, CAP, part_width), BF16),
+            pltpu.VMEM((fronts, CHUNKS, PLANES, CAP, part_width), BF16),
             pltpu.VMEM((GROUP, fronts, RING * slots, units), BF16),
             pltpu.VMEM((units, GROUP * units), F32),
             dma((3,)), dma((fronts,)), dma((fronts,)), dma,
             dma, dma,
-            dma((fronts, PLANES)),
-            dma((fronts, PLANES)), dma((fronts, PLANES)),
+            dma((fronts, CHUNKS, PLANES)),
+            dma((fronts, CHUNKS, PLANES)), dma((fronts, CHUNKS, PLANES)),
+            dma((fronts, CHUNKS, RING)), dma((fronts, CHUNKS, RING)),
             dma((fronts, RING)), dma((fronts, RING)),
             dma((fronts, GROUP)), dma((fronts, GROUP)),
-            dma((fronts, RING)), dma((fronts, RING)),
-            dma((fronts, PLANES)), dma((fronts, PLANES)),
+            dma((fronts, CHUNKS, RING)), dma((fronts, CHUNKS, RING)),
+            dma((fronts, CHUNKS, PLANES)), dma((fronts, CHUNKS, PLANES)),
             dma((fronts,)), dma((fronts,)),
         ],
         compiler_params=pltpu.CompilerParams(
-            collective_id=0, has_side_effects=True, vmem_limit_bytes=48 * 1024 * 1024
+            collective_id=0, has_side_effects=True, vmem_limit_bytes=60 * 1024 * 1024
         ),
     )(stream_in, gain, w_gate, w_up, w_down, route_cols, gate_cols)
 

time: 274 us -> 247 us (0.901)
  Pallas kernels: 263 us -> 241 us
  local copies, waits for them, and re-layouts: 10.4 us -> 5.3 us
    pallas_call x1, Pallas kernels: 263 us -> 241 us  [shards(): pl.pallas_call(kernel, out_shape=(jax.ShapeDtypeStruct((1, fronts, tokens...]
    unnamed x14 -> x2, local copies, waits for them, and re-layouts: 10.4 us -> 5.3 us
where the time goes in v2:
time: 247 us
  Pallas kernels  241 us (98%)
  local copies, waits for them, and re-layouts  5.3 us (2%)
    pallas_call x1, Pallas kernels, shards(): pl.pallas_call(kernel, out_shape=(jax.ShapeDtypeStruct((1, fronts, tokens...  241 us
    unnamed x2, local copies, waits for them, and re-layouts  5.3 us

profile of v2, /device:TPU:25, one launch (start us, length us, event | category | flops | bytes accessed | tf_op | source)
XLA Modules:
  0.0 247.0 jit_solution(9499493295440810442)
XLA Ops:
  0.6 241.1 %shard_map.86 = (bf16[1,4,32,3584]{3,2,1,0:T(8,128)(2,1)}, f32[1,256,2048]{2,1,0:T(8,128)}) custom-call(bf16[4,32,3584]{2,1,0:T(8,128)(2,1)} %stream.1, f32[1,3584]{1,0:T(1,128)} %gain.1, bf16[1,3584,256]{2,1,0:T(8,128)(2,1)} %wg.1, bf16[1,3584,256]{2,1,0:T(8,128)(2,1)} %wu.1, bf16[1,256,3584]{2,1,0:T(8,128)(2,1)} %wd.1, s32[4,8,32]{2,1,0:T(8,128)} %bitcast.6, ...), custom_call_target="tpu_custom_call" | custom-call | tf_op jit(solution)/shard_map/pallas_call | solution.py:399
  241.7 2.2 copy.11
  243.9 3.1 %copy.12 = f32[1,256,2048]{2,1,0:T(8,128)} copy(f32[1,256,2048]{2,1,0:T(8,128)} %get-tuple-element.5) | data formatting | bytes 4194304

commit v3 on v2

--- a/solution.py
+++ b/solution.py
@@ -52,17 +52,7 @@
     def at_x(step):
         return lax.rem(x + step, RING)
 
-    def peers():
-        group = []
-        for other in (0, 1):
-            for step in range(RING):
-                if other or step:
-                    p = lax.rem(half + other, 2)
-                    nx = at_x(step)
-                    group.append(((z - half + p) * RING + nx, p * RING + nx))
-        return group
-
-    group = peers()
+    opposite = (z - half + (1 - half)) * RING + x
 
     def remote(src, dst, send, recv, to_layer, to_place):
         return pltpu.make_async_remote_copy(
@@ -89,8 +79,8 @@
         return remote(scales.at[f, slot], scales.at[f, slot],
                       c_send.at[f, to_x], c_recv.at[f, slot], layer, z * RING + to_x)
 
-    def copy_h(f, to_place, to_member, slot):
-        return remote(hid.at[slot, f], hid.at[slot, f], h_send.at[f, to_member], h_recv.at[f, slot],
+    def copy_h(f, to_place, slot, number):
+        return remote(hid.at[slot, f], hid.at[slot, f], h_send.at[f, number], h_recv.at[f, slot],
                       layer, to_place)
 
     def copy_d(f, c, to_x, slot):
@@ -145,8 +135,6 @@
         greet(layer, at_z(step) * RING + x)
     for step in range(1, RING):
         greet(layer, z * RING + at_x(step))
-    for step in range(1, RING):
-        greet(layer, (z - half + (1 - half)) * RING + at_x(step))
 
     lanes = lax.broadcasted_iota(jnp.int32, (1, tokens), 1)
     row8 = lax.broadcasted_iota(jnp.int32, (flight * CAP, tokens), 0)
@@ -189,19 +177,19 @@
 
     @pl.when(jnp.logical_and(is_first, is_last))
     def _():
-        pl.semaphore_wait(barrier, 13)
+        pl.semaphore_wait(barrier, 10)
 
     @pl.when(jnp.logical_and(is_first, jnp.logical_not(is_last)))
     def _():
-        pl.semaphore_wait(barrier, 13 + PLANES)
+        pl.semaphore_wait(barrier, 10 + PLANES)
 
     @pl.when(jnp.logical_and(jnp.logical_not(is_first), is_last))
     def _():
-        pl.semaphore_wait(barrier, 13 + 1)
+        pl.semaphore_wait(barrier, 10 + 1)
 
     @pl.when(jnp.logical_and(jnp.logical_not(is_first), jnp.logical_not(is_last)))
     def _():
-        pl.semaphore_wait(barrier, 13 + 1 + PLANES)
+        pl.semaphore_wait(barrier, 10 + 1 + PLANES)
 
     @pl.when(layer > 0)
     def _():
@@ -256,8 +244,15 @@
             for step in (2, 1, 3):
                 copy_d(f, c, at_x(step), x).start()
         hid[member, f] = hidden
-        for to_place, to_member in group:
-            copy_h(f, to_place, to_member, member).start()
+        copy_h(f, opposite, member, PLANES).start()
+        for step in (2, 1, 3):
+            copy_h(f, z * RING + at_x(step), half * RING + x, at_x(step)).start()
+
+    def stage_h(f):
+        for step in range(1, RING):
+            slot = half * RING + at_x(step)
+            copy_h(f, place, slot, PLANES).wait_recv()
+            copy_h(f, opposite, slot, PLANES + step).start()
 
     def stage_d(f):
         for c in range(chunks):
@@ -328,26 +323,31 @@
         stage_d(f)
         stage_a(f + 1)
         stage_e(f)
+        stage_h(f)
         stage_b(f + 1)
         return carry
 
     lax.fori_loop(0, fronts - 1, steady, 0)
-    stage_d(fronts - 1)
-
-    for f in range(fronts):
-        for _, slot in group:
-            copy_h(f, place, member, slot).wait_recv()
-    mine = hid[member].reshape(-1, hid.shape[-1])
-    units = hid.shape[-1]
-    for slot in range(GROUP):
-        theirs = hid[slot].reshape(-1, units)
-        gram[:, slot * units:(slot + 1) * units] = lax.dot_general(
-            mine, theirs, (((0,), (0,)), ((), ())), preferred_element_type=F32
-        ) * (1.0 / (fronts * CAP))
     store_gram = pltpu.make_async_copy(gram, hess.at[0], hess_sem)
-    store_gram.start()
-
-    stage_e(fronts - 1)
+
+    def stage_gram():
+        for f in range(fronts):
+            for column in range(RING):
+                copy_h(f, place, (1 - half) * RING + column, PLANES).wait_recv()
+        mine = hid[member].reshape(-1, hid.shape[-1])
+        units = hid.shape[-1]
+        for slot in range(GROUP):
+            theirs = hid[slot].reshape(-1, units)
+            gram[:, slot * units:(slot + 1) * units] = lax.dot_general(
+                mine, theirs, (((0,), (0,)), ((), ())), preferred_element_type=F32
+            ) * (1.0 / (fronts * CAP))
+        store_gram.start()
+
+    last = fronts - 1
+    stage_d(last)
+    stage_h(last)
+    stage_e(last)
+    stage_gram()
 
     @pl.when(layer > 0)
     def _():
@@ -356,8 +356,10 @@
     def finish(f, carry):
         for step in range(1, RING):
             copy_c(f, at_x(step), x).wait_send()
-        for to_place, to_member in group:
-            copy_h(f, to_place, to_member, member).wait_send()
+        copy_h(f, opposite, member, PLANES).wait_send()
+        for step in range(1, RING):
+            copy_h(f, place, member, at_x(step)).wait_send()
+            copy_h(f, opposite, member, PLANES + step).wait_send()
         for c in range(chunks):
             for step in range(1, RING):
                 copy_b(f, c, at_x(step), x).wait_send()
@@ -431,7 +433,7 @@
             dma((fronts, CHUNKS, PLANES)), dma((fronts, CHUNKS, PLANES)),
             dma((fronts, CHUNKS, RING)), dma((fronts, CHUNKS, RING)),
             dma((fronts, RING)), dma((fronts, RING)),
-            dma((fronts, GROUP)), dma((fronts, GROUP)),
+            dma((fronts, PLANES + RING)), dma((fronts, GROUP)),
             dma((fronts, CHUNKS, RING)), dma((fronts, CHUNKS, RING)),
             dma((fronts, CHUNKS, PLANES)), dma((fronts, CHUNKS, PLANES)),
             dma((fronts,)), dma((fronts,)),

time: 247 us -> 238 us (0.964)
  Pallas kernels: 241 us -> 232 us
    pallas_call x1, Pallas kernels: 241 us -> 232 us  [shards(): pl.pallas_call(kernel, out_shape=(jax.ShapeDtypeStruct((1, fronts, tokens...]
where the time goes in v3:
time: 238 us
  Pallas kernels  232 us (97%)
  local copies, waits for them, and re-layouts  5.3 us (2%)
    pallas_call x1, Pallas kernels, shards(): pl.pallas_call(kernel, out_shape=(jax.ShapeDtypeStruct((1, fronts, tokens...  232 us
    unnamed x2, local copies, waits for them, and re-layouts  5.3 us

profile of v3, /device:TPU:25, one launch (start us, length us, event | category | flops | bytes accessed | tf_op | source)
XLA Modules:
  0.0 238.2 jit_solution(7918793279337720300)
XLA Ops:
  0.6 232.3 %shard_map.86 = (bf16[1,4,32,3584]{3,2,1,0:T(8,128)(2,1)}, f32[1,256,2048]{2,1,0:T(8,128)}) custom-call(bf16[4,32,3584]{2,1,0:T(8,128)(2,1)} %stream.1, f32[1,3584]{1,0:T(1,128)} %gain.1, bf16[1,3584,256]{2,1,0:T(8,128)(2,1)} %wg.1, bf16[1,3584,256]{2,1,0:T(8,128)(2,1)} %wu.1, bf16[1,256,3584]{2,1,0:T(8,128)(2,1)} %wd.1, s32[4,8,32]{2,1,0:T(8,128)} %bitcast.6, ...), custom_call_target="tpu_custom_call" | custom-call | tf_op jit(solution)/shard_map/pallas_call | solution.py:401
  232.9 2.2 copy.11
  235.1 3.1 %copy.12 = f32[1,256,2048]{2,1,0:T(8,128)} copy(f32[1,256,2048]{2,1,0:T(8,128)} %get-tuple-element.5) | data formatting | bytes 4194304

commit v4 on v3

--- a/solution.py
+++ b/solution.py
@@ -216,12 +216,12 @@
 
             wide = arecv[f, c].reshape(PLANES * CAP, part_width).astype(F32)
             rows[f, c, x] = (wide * gain[:, columns(c)]).astype(BF16)
-            for step in (2, 1, 3):
+            for step in (1, 3, 2):
                 copy_b(f, c, at_x(step), x).start()
             squares = squares + jnp.sum(wide * wide, axis=-1, keepdims=True)
         scale = lax.rsqrt(squares * (1.0 / width) + EPSILON)
         scales[f, x] = jnp.broadcast_to(scale, scales.shape[2:])
-        for step in (2, 1, 3):
+        for step in (1, 3, 2):
             copy_c(f, at_x(step), x).start()
 
     def stage_b(f):
@@ -241,11 +241,11 @@
         for c in range(chunks):
             partial = jnp.dot(hidden, wd_v[:, columns(c)], preferred_element_type=F32)
             part[f, c] = partial.astype(BF16).reshape(RING, PLANES * CAP, part_width)
-            for step in (2, 1, 3):
+            for step in (1, 3, 2):
                 copy_d(f, c, at_x(step), x).start()
         hid[member, f] = hidden
         copy_h(f, opposite, member, PLANES).start()
-        for step in (2, 1, 3):
+        for step in (1, 3, 2):
             copy_h(f, z * RING + at_x(step), half * RING + x, at_x(step)).start()
 
     def stage_h(f):
@@ -266,29 +266,30 @@
                 copy_e(f, c, at_z(step), z).start()
             erecv[f, c, z] = ebuf[f, c, z]
 
+    def stack(f, c):
+        returned = erecv[f, c].reshape(PLANES * CAP, part_width)
+        return jnp.concatenate([xin[f, :, columns(c)], returned, returned], axis=0)
+
     def stage_e(f):
         @pl.when(layer > 0)
         def _():
             copy_x(f, layer).wait_recv()
 
-        def stack(c):
-            returned = erecv[f, c].reshape(PLANES * CAP, part_width)
-            return jnp.concatenate([xin[f, :, columns(c)], returned, returned], axis=0)
-
         for c in range(chunks):
             for step in range(1, PLANES):
                 copy_e(f, c, z, at_z(step)).wait_recv()
 
             @pl.when(layer < sections - 1)
             def _():
-                picked = jnp.dot(mix_next[f], stack(c), preferred_element_type=F32)
+                picked = jnp.dot(mix_next[f], stack(f, c), preferred_element_type=F32)
                 abuf[f, c] = picked.astype(BF16).reshape(flight, CAP, part_width)
                 for step in range(PLANES):
                     copy_a(f, c, at_z(step), z, layer + 1).start()
 
+    def stage_u(f):
         for c in range(chunks):
             xout[f, :, columns(c)] = jnp.dot(
-                mix_full[f], stack(c), preferred_element_type=F32
+                mix_full[f], stack(f, c), preferred_element_type=F32
             ).astype(BF16)
 
         @pl.when(layer < sections - 1)
@@ -325,6 +326,7 @@
         stage_e(f)
         stage_h(f)
         stage_b(f + 1)
+        stage_u(f)
         return carry
 
     lax.fori_loop(0, fronts - 1, steady, 0)
@@ -347,6 +349,7 @@
     stage_d(last)
     stage_h(last)
     stage_e(last)
+    stage_u(last)
     stage_gram()
 
     @pl.when(layer > 0)

time: 238 us -> 240 us (level)
  no operation moved by 1% of the time
where the time goes in v4:
time: 240 us
  Pallas kernels  234 us (98%)
  local copies, waits for them, and re-layouts  5.3 us (2%)
    pallas_call x1, Pallas kernels, shards(): pl.pallas_call(kernel, out_shape=(jax.ShapeDtypeStruct((1, fronts, tokens...  234 us
    unnamed x2, local copies, waits for them, and re-layouts  5.3 us

profile of v4, /device:TPU:25, one launch (start us, length us, event | category | flops | bytes accessed | tf_op | source)
XLA Modules:
  0.0 240.3 jit_solution(12178236626267604556)
XLA Ops:
  0.6 234.3 %shard_map.86 = (bf16[1,4,32,3584]{3,2,1,0:T(8,128)(2,1)}, f32[1,256,2048]{2,1,0:T(8,128)}) custom-call(bf16[4,32,3584]{2,1,0:T(8,128)(2,1)} %stream.1, f32[1,3584]{1,0:T(1,128)} %gain.1, bf16[1,3584,256]{2,1,0:T(8,128)(2,1)} %wg.1, bf16[1,3584,256]{2,1,0:T(8,128)(2,1)} %wu.1, bf16[1,256,3584]{2,1,0:T(8,128)(2,1)} %wd.1, s32[4,8,32]{2,1,0:T(8,128)} %bitcast.6, ...), custom_call_target="tpu_custom_call" | custom-call | tf_op jit(solution)/shard_map/pallas_call | solution.py:404
  235.0 2.2 copy.11
  237.1 3.1 %copy.12 = f32[1,256,2048]{2,1,0:T(8,128)} copy(f32[1,256,2048]{2,1,0:T(8,128)} %get-tuple-element.5) | data formatting | bytes 4194304
